TPU v7x, 32 devices: a whole 2x2x4 slice. The times are simulated.
32 devices in a mesh: parts: 2 (over x), tp: 16 (over z, y, core).
Axes of the slice: x: 2, y: 2, z: 4, core: 2. Of those that a mesh axis runs over, the one named last changes fastest.
Arguments:
- queries: bfloat16 [64, 16384], P(('parts', 'tp')), parts along dimension 0, may hold values from -40 to 40
- new_token_key_value: bfloat16 [64, 2048], P(('parts', 'tp')), parts along dimension 0, may hold values from -6 to 6
- key_value_cache: bfloat16 [2048, 16, 2048], P(('parts', 'tp')), parts along dimension 0, may hold values from -40 to 40
- row_page_table: int32 [64, 32], P(('parts', 'tp')), parts along dimension 0, may hold values from 0 to 63, as said below
- lengths: int32 [64], P(('parts', 'tp')), parts along dimension 0, may hold values from 1 to 512, as said below
- output_weight_matrix: bfloat16 [16384, 16384], P('tp'), may hold values from -0.0625 to 0.0625
- row_adapter_index: int32 [64, 1], P('parts'), parts along dimension 0, may hold values from 0 to 15; in each aligned block of 32 rows (0 to 31, 32 to 63, ...) at most 4 rows name the same one
- adapter_storage_index: int32 [32], P('parts'), parts along dimension 0, may hold values from 0 to 15, each once
- adapter_down_factor: bfloat16 [32, 64, 16384], P(('parts', 'tp')), parts along dimension 0, may hold values from -0.046875 to 0.046875
- adapter_up_factor: bfloat16 [32, 64, 16384], P(('parts', 'tp')), parts along dimension 0, may hold values from -0.75 to 0.75
Outputs:
- mixed: bfloat16 [64, 16384], P('parts', 'tp'), parts along dimension 0
There are 2 independent parts, one for each index of `parts`. A program takes and returns all parts, laid end to end along the dimension named above; an argument that names none is the same for every part. Nothing has to cross between parts.
Inputs may be any that keep to these rules, and one draw needn't show every extreme that they name: `row_page_table`: the rows held by one device use distinct pages of that device's pool of 64 pages, and every page of the pool. `lengths`: some row has exactly 512 cached tokens. `row_adapter_index`: at most 4 rows name one adapter, a bound that some block reaches; every adapter is named by some row. A permutation: adapter a's factors stand at index adapter_storage_index[a] of adapter_down_factor and adapter_up_factor.
All inputs are finite; a program needn't handle non-finite values.
Results may differ from a plain program's by a relative error of at most 0.009.
Values may be sent and summed in bfloat16 or wider, within the bound.
A program may use at most 128 MiB of HBM per device.

v0:
```python
import jax
import jax.numpy as jnp
from jax import lax
from jax.sharding import PartitionSpec as P

QUERY_HEADS = 128
KVH = 8
HEAD_SIZE = 128
PAGE = 16
MAXP = 32


adapter_scale = 2.0


def attend_rows(queries, new_token_key_value, gathered_pages, lengths):
    local_rows = queries.shape[0]
    token_count = MAXP * PAGE
    group_size = QUERY_HEADS // KVH
    grouped = queries.reshape(local_rows, KVH, group_size, HEAD_SIZE)
    cached = gathered_pages.reshape(local_rows, token_count, KVH, 2, HEAD_SIZE)
    fresh = new_token_key_value.reshape(local_rows, KVH, 2, HEAD_SIZE)
    scale_factor = HEAD_SIZE ** (-0.5)
    scores = (
        jnp.einsum(
            "rkgh,rlkh->rkgl", grouped, cached[:, :, :, 0, :], preferred_element_type=jnp.float32
        )
        * scale_factor
    )
    fresh_score = (
        jnp.einsum("rkgh,rkh->rkg", grouped, fresh[:, :, 0, :], preferred_element_type=jnp.float32)
        * scale_factor
    )
    position = jnp.arange(token_count, dtype=jnp.int32)
    visible = position[None, :] < lengths[:, None]
    scores = jnp.where(visible[:, None, None, :], scores, -1e30)
    row_max = jnp.maximum(jnp.max(scores, axis=-1), fresh_score)
    cached_exp = jnp.exp(scores - row_max[..., None])
    fresh_exp = jnp.exp(fresh_score - row_max)
    total = jnp.sum(cached_exp, axis=-1) + fresh_exp
    weights = (cached_exp / total[..., None]).astype(jnp.bfloat16)
    fresh_weight = (fresh_exp / total).astype(jnp.bfloat16)
    output = jnp.einsum(
        "rkgl,rlkh->rkgh", weights, cached[:, :, :, 1, :], preferred_element_type=jnp.float32
    )
    output = output + fresh_weight.astype(jnp.float32)[..., None] * fresh[:, :, None, 1, :].astype(
        jnp.float32
    )
    return output.reshape(local_rows, QUERY_HEADS * HEAD_SIZE).astype(jnp.bfloat16)


def body(
    queries,
    new_token_key_value,
    key_value_cache,
    row_page_table,
    lengths,
    output_weight_matrix,
    row_adapter_index,
    adapter_storage_index,
    adapter_down_factor,
    adapter_up_factor,
):
    gathered_pages = key_value_cache[row_page_table]
    attention_output = attend_rows(queries, new_token_key_value, gathered_pages, lengths)
    head_rows = lax.all_to_all(attention_output, "tp", split_axis=1, concat_axis=0, tiled=True)
    partial_value = jnp.dot(head_rows, output_weight_matrix, preferred_element_type=jnp.float32)
    base_projection = lax.psum_scatter(partial_value, "tp", scatter_dimension=1, tiled=True)
    row_adapter = row_adapter_index[:, 0]
    row_owner = adapter_storage_index[row_adapter]
    down_slices, up_slices = (
        lax.all_to_all(adapter_down_factor, "tp", split_axis=2, concat_axis=0, tiled=True),
        lax.all_to_all(adapter_up_factor, "tp", split_axis=2, concat_axis=0, tiled=True),
    )
    picked = down_slices[row_owner]
    partial_low = jnp.einsum("rh,rkh->rk", head_rows, picked, preferred_element_type=jnp.float32)
    reduced_output = lax.psum(partial_low, "tp").astype(jnp.bfloat16)
    adapter_term = jnp.einsum(
        "rk,rkd->rd", reduced_output, up_slices[row_owner], preferred_element_type=jnp.float32
    )
    adapter_delta = (adapter_scale * adapter_term).astype(jnp.bfloat16)
    return (base_projection + adapter_delta.astype(jnp.float32)).astype(jnp.bfloat16)


def solution(mesh):
    in_specs = (
        P(("parts", "tp"), None),
        P(("parts", "tp"), None),
        P(("parts", "tp"), None, None),
        P(("parts", "tp"), None),
        P(("parts", "tp")),
        P("tp", None),
        P("parts", None),
        P("parts"),
        P(("parts", "tp"), None, None),
        P(("parts", "tp"), None, None),
    )
    out_specs = P("parts", "tp")
    return jax.shard_map(body, mesh=mesh, in_specs=in_specs, out_specs=out_specs, check_vma=False)
```

profile of v0, /device:TPU:0, one launch (start us, length us, event | category | flops | bytes accessed | tf_op | source)
XLA Modules:
  0.0 440.8 jit_solution(17846975777799738143)
XLA Ops:
  7.3 5.0 %gather_fusion = bf16[64,16,2048]{2,1,0:T(8,128)(2,1)} fusion(bf16[64,16,2048]{2,1,0:T(8,128)(2,1)} %param.12, s32[1024]{0:T(1024)S(1)} %pad_clamp_fusion.2), kind=kCustom, calls=%fused_computation | custom fusion | bytes 8388864 | tf_op jit(solution)/shard_map/gather | solution.py:64
  12.3 7.7 %reshape.48 = bf16[2,512,8,2,128]{4,3,2,1,0:T(2,128)(2,1)} reshape(bf16[64,16,2048]{2,1,0:T(8,128)(2,1)} %gather_fusion) | data formatting | bytes 8388608 | tf_op jit(solution)/shard_map/reshape | solution.py:21
  20.0 10.0 %fusion.18 = (bf16[2,512,8,1,128]{4,3,2,1,0:T(2,128)(2,1)}, bf16[2,512,8,1,128]{4,3,2,1,0:T(2,128)(2,1)}) fusion(bf16[2,512,8,2,128]{4,3,2,1,0:T(2,128)(2,1)} %reshape.48), kind=kLoop, calls=%fused_computation.41 | loop fusion | bytes 8388608 | tf_op jit(solution)/shard_map/slice | solution.py:26
  30.3 3.4 fusion.19
  38.0 7.4 %all-to-all-start = ((bf16[2,16,1024]{2,0,1:T(2,128)(2,1)}), bf16[2,16,1024]{2,0,1:T(2,128)(2,1)S(1)}, u32[]{:S(2)}, u32[]{:S(2)}) async-start(bf16[2,16,1024]{2,0,1:T(2,128)(2,1)} %copy.22), calls=%async_computation | async-start | bytes 131072 | tf_op jit(solution)/shard_map/all_to_all | solution.py:66
  45.4 12.9 %copy.23 = bf16[1,64,16384]{1,0,2:T(2,128)(2,1)} copy(bf16[1,64,16384]{2,1,0:T(8,128)(2,1)S(1)} %copy-done.1) | data formatting | bytes 4194304 | tf_op args[8]
  58.9 90.8 %reduce.1 = bf16[16384,64]{1,0:T(8,128)(2,1)} reduce(bf16[16384,1,64]{2,1,0:T(2,128)(2,1)} %bitcast.68, bf16[]{:T(256)} %broadcast.59), dimensions={1}, to_apply=%bitcast.57.reduce_sub_computation | reduce | bytes 4194306
  149.7 7.5 %reshape.100 = bf16[16,2,32768]{2,1,0:T(2,128)(2,1)} reshape(bf16[16384,64]{1,0:T(8,128)(2,1)} %reduce.1) | data formatting | bytes 4194304
  157.3 6.0 %all-to-all-start.1 = ((bf16[16,2,32768]{2,1,0:T(2,128)(2,1)}), bf16[16,2,32768]{2,1,0:T(2,128)(2,1)S(1)}, u32[]{:S(2)}, u32[]{:S(2)}) async-start(bf16[16,2,32768]{2,1,0:T(2,128)(2,1)} %reshape.100), calls=%async_computation.2 | async-start | bytes 4194304 | tf_op jit(solution)/shard_map/all_to_all | solution.py:72
  163.3 17.2 %copy.26 = bf16[1,64,16384]{1,0,2:T(2,128)(2,1)} copy(bf16[1,64,16384]{2,1,0:T(8,128)(2,1)} %param.19) | data formatting | bytes 4194304 | tf_op args[9]
  180.5 90.8 %reduce = bf16[16384,64]{1,0:T(8,128)(2,1)} reduce(bf16[16384,1,64]{2,1,0:T(2,128)(2,1)} %bitcast.69, bf16[]{:T(256)} %broadcast.59), dimensions={1}, to_apply=%bitcast.55.reduce_sub_computation | reduce | bytes 4194306
  271.3 7.5 %reshape.98 = bf16[16,2,32768]{2,1,0:T(2,128)(2,1)} reshape(bf16[16384,64]{1,0:T(8,128)(2,1)} %reduce) | data formatting | bytes 4194304
  278.9 6.1 %all-to-all-start.2 = ((bf16[16,2,32768]{2,1,0:T(2,128)(2,1)}), bf16[16,2,32768]{2,1,0:T(2,128)(2,1)}, u32[]{:S(2)}, u32[]{:S(2)}) async-start(bf16[16,2,32768]{2,1,0:T(2,128)(2,1)} %reshape.98), calls=%async_computation.3 | async-start | bytes 4194304 | tf_op jit(solution)/shard_map/all_to_all | solution.py:73
  285.2 14.9 %fusion.20 = f32[32,16384]{1,0:T(8,128)} fusion(bf16[32,1024]{1,0:T(8,128)(2,1)S(1)} %all_to_all.40, bf16[1024,16384]{1,0:T(8,128)(2,1)} %param.15), kind=kOutput, calls=%fused_computation.43 | convolution fusion | flops 1073741824 | bytes 35717120 | tf_op jit(solution)/shard_map/dot_general | solution.py:67
  301.0 8.4 %reshape.101 = bf16[16384,1,64]{2,1,0:T(2,128)(2,1)} reshape(bf16[16,2,32768]{2,1,0:T(2,128)(2,1)S(1)} %all-to-all-done.1) | data formatting | bytes 4194304
  309.4 6.1 %copy.39 = bf16[1,64,16384]{1,2,0:T(8,128)(2,1)} copy(bf16[1,64,16384]{1,0,2:T(2,128)(2,1)} %bitcast.70) | data formatting | bytes 4194304
  315.5 3.6 copy.25
  319.1 7.0 %all-to-all-done.2 = bf16[16,2,32768]{2,1,0:T(2,128)(2,1)} async-done(((bf16[16,2,32768]{2,1,0:T(2,128)(2,1)}), bf16[16,2,32768]{2,1,0:T(2,128)(2,1)}, u32[]{:S(2)}, u32[]{:S(2)}) %all-to-all-start.2) | async-done | bytes 2097184 | tf_op jit(solution)/shard_map/all_to_all | solution.py:73
  326.1 11.8 %reshape.99 = bf16[16384,1,64]{2,1,0:T(2,128)(2,1)} reshape(bf16[16,2,32768]{2,1,0:T(2,128)(2,1)} %all-to-all-done.2) | data formatting | bytes 4194304
  338.0 5.9 %copy.40 = bf16[1,64,16384]{1,2,0:T(8,128)(2,1)} copy(bf16[1,64,16384]{1,0,2:T(2,128)(2,1)} %bitcast.71) | data formatting | bytes 4194304
  343.9 4.8 %copy.28 = bf16[1,64,16,1024]{3,1,2,0:T(8,128)(2,1)} copy(bf16[1,64,16,1024]{1,3,2,0:T(8,128)(2,1)} %bitcast.75) | data formatting | bytes 4194304 | tf_op jit(solution)/shard_map/all_to_all | solution.py:73
  351.5 4.4 gather_fusion.3
  355.8 3.4 fusion.21
  359.2 70.3 %psum.7 = bf16[32,64]{1,0:T(8,128)(2,1)S(1)} all-reduce(f32[32,64]{1,0:T(8,128)S(1)} %bitcast.84), channel_id=1, replica_groups=mesh['parts'=2,'tp'=16] {'tp'}, use_global_device_ids=true, to_apply=%region_3.4 | all-reduce | flops 2048 | bytes 12288 | tf_op jit(solution)/shard_map/psum | solution.py:77
  (42 shorter events, 14.2 us)
Async XLA Ops:
  6.5 293.6 %copy-start = (s32[16]{0:T(128)S(1)}, s32[16]{0:T(128)}, u32[]{:S(2)}) copy-start(s32[16]{0:T(128)} %param.17) | copy-start | bytes 196
  20.0 10.0 %copy-start.2 = (bf16[2,16384]{1,0:T(2,128)(2,1)S(1)}, bf16[2,16384]{1,0:T(2,128)(2,1)}, u32[]{:S(2)}) copy-start(bf16[2,16384]{1,0:T(2,128)(2,1)} %param.10) | copy-start | bytes 196612
  20.0 10.0 %copy-start.4 = (s32[2]{0:T(128)S(1)}, s32[2]{0:T(128)}, u32[]{:S(2)}) copy-start(s32[2]{0:T(128)} %param.14) | copy-start | bytes 28
  20.0 10.1 %copy-start.3 = (bf16[2,2048]{1,0:T(2,128)(2,1)S(1)}, bf16[2,2048]{1,0:T(2,128)(2,1)}, u32[]{:S(2)}) copy-start(bf16[2,2048]{1,0:T(2,128)(2,1)} %param.11) | copy-start | bytes 24580
  30.3 15.2 %copy-start.1 = (bf16[1,64,16384]{2,1,0:T(8,128)(2,1)S(1)}, bf16[1,64,16384]{2,1,0:T(8,128)(2,1)}, u32[]{:S(2)}) copy-start(bf16[1,64,16384]{2,1,0:T(8,128)(2,1)} %param.18) | copy-start | bytes 6291460
  38.0 119.2 %all-to-all-start = ((bf16[2,16,1024]{2,0,1:T(2,128)(2,1)}), bf16[2,16,1024]{2,0,1:T(2,128)(2,1)S(1)}, u32[]{:S(2)}, u32[]{:S(2)}) async-start(bf16[2,16,1024]{2,0,1:T(2,128)(2,1)} %copy.22), calls=%async_computation | async-start | bytes 131072 | tf_op jit(solution)/shard_map/all_to_all | solution.py:66
  157.3 121.6 %all-to-all-start.1 = ((bf16[16,2,32768]{2,1,0:T(2,128)(2,1)}), bf16[16,2,32768]{2,1,0:T(2,128)(2,1)S(1)}, u32[]{:S(2)}, u32[]{:S(2)}) async-start(bf16[16,2,32768]{2,1,0:T(2,128)(2,1)} %reshape.100), calls=%async_computation.2 | async-start | bytes 4194304 | tf_op jit(solution)/shard_map/all_to_all | solution.py:72
  278.9 47.2 %all-to-all-start.2 = ((bf16[16,2,32768]{2,1,0:T(2,128)(2,1)}), bf16[16,2,32768]{2,1,0:T(2,128)(2,1)}, u32[]{:S(2)}, u32[]{:S(2)}) async-start(bf16[16,2,32768]{2,1,0:T(2,128)(2,1)} %reshape.98), calls=%async_computation.3 | async-start | bytes 4194304 | tf_op jit(solution)/shard_map/all_to_all | solution.py:73
  285.0 15.2 %copy-start.5 = (s32[32,1]{0,1:T(1,128)S(1)}, s32[32,1]{0,1:T(1,128)}, u32[]{:S(2)}) copy-start(s32[32,1]{0,1:T(1,128)} %param.16) | copy-start | bytes 388
  285.0 147.4 %reduce-scatter.2.cloned.1.call-start = ((), (), s32[]{:S(2)}) async-start(), calls=%async_computation.4 | async-start | bytes 2228224 | tf_op jit(solution)/shard_map/reduce_scatter | solution.py:68
Sparse Core Ops, SparseCore 0:
  300.3 64.5 reduce-scatter.1
where the time goes:
time: 443 us; the launch traced here: 441 us
  other arithmetic  184 us (42%)
  local copies, waits for them, and re-layouts  118 us (27%)
  blocking collectives  70.3 us (16%)
  matrix products  28 us (6%)
  starting transfers between devices  19.7 us (4%)
  between operations  13.6 us (3%)
  waiting for transfers between devices  7.05 us (2%)
    unnamed x2, other arithmetic  182 us
    unnamed x22, local copies, waits for them, and re-layouts  78 us
    psum x1, blocking collectives, body(): reduced_output = lax.psum(partial_low, 'tp').astype(jnp.bfloat16)  70.3 us
    dot_general x1, matrix products, body(): jnp.dot(head_rows, output_weight_matrix, preferred_element_type=jnp.float32)  14.9 us
    slice x1, local copies, waits for them, and re-layouts, attend_rows(): cached[:, :, :, 0, :]  10 us
  transfers between devices with their start and end apart: 4, of which 1 were waited for; matrix products, arithmetic and copies ran while one was open for 67% of the time, Pallas kernels for 0%

commit v1 on v0

--- a/solution.py
+++ b/solution.py
@@ -1,6 +1,10 @@
+import functools
+
 import jax
 import jax.numpy as jnp
 from jax import lax
+from jax.experimental import pallas as pl
+from jax.experimental.pallas import tpu as pltpu
 from jax.sharding import PartitionSpec as P
 
 QUERY_HEADS = 128
@@ -8,9 +12,401 @@
 HEAD_SIZE = 128
 PAGE = 16
 MAXP = 32
+CAP = 4
+MESH = pl.DeviceIdType.MESH
 
 
 adapter_scale = 2.0
+
+
+def fused_kernel(
+    n,
+    q_ref,
+    new_ref,
+    kv_hbm,
+    table_ref,
+    len_ref,
+    w_hbm,
+    adapter_ref,
+    storage_ref,
+    down_hbm,
+    up_hbm,
+    out_ref,
+    kv,
+    w,
+    down,
+    up,
+    bias,
+    send1,
+    recv1,
+    xf,
+    xs,
+    send2,
+    recv2,
+    send3,
+    recv3,
+    psend,
+    precv,
+    keep,
+    isend,
+    irecv,
+    kv_sem,
+    w_sem,
+    f_sem,
+    ss1,
+    rs1,
+    ss2,
+    rs2,
+    ss3,
+    rs3,
+    pss,
+    prs,
+    iss,
+    irs,
+):
+    f32, bf16, i32 = jnp.float32, jnp.bfloat16, jnp.int32
+    part = lax.axis_index("parts")
+    me = lax.axis_index("tp")
+    core = lax.rem(me, 2)
+    chip = lax.div(me, 2)
+    chips = n // 2
+    tokens = kv.shape[1]
+    rows = xs.shape[0]
+    width = xs.shape[1]
+
+    def to_chip(k):
+        return lax.rem(chip + k + 1, chips)
+
+    def kv_copy(g):
+        return pltpu.make_async_copy(
+            kv_hbm.at[:, pl.ds(pl.multiple_of(g * 256, 256), 256)], kv.at[g], kv_sem.at[g]
+        )
+
+    def w_copy(i):
+        k, own = lax.div(i, 2), lax.rem(i, 2)
+        device = to_chip(k) * 2 + jnp.where(own == 1, core, 1 - core)
+        start = pl.multiple_of(device * width, width)
+        return pltpu.make_async_copy(w_hbm.at[:, pl.ds(start, width)], w.at[i], w_sem.at[i])
+
+    down_copy = pltpu.make_async_copy(down_hbm, down, f_sem.at[0])
+    up_copy = pltpu.make_async_copy(up_hbm, up, f_sem.at[1])
+
+    def loop(low, high, body):
+        lax.fori_loop(low, high, lambda i, c: (body(i), c)[1], 0)
+
+    def to_peers(body):
+        def one(d):
+            @pl.when(d != me)
+            def _():
+                body(d)
+
+        loop(0, n, one)
+
+    loop(0, KVH, lambda g: kv_copy(g).start())
+    loop(0, 8, lambda i: w_copy(i).start())
+    down_copy.start()
+    up_copy.start()
+    loop(8, n, lambda i: w_copy(i).start())
+
+    barrier = pltpu.get_barrier_semaphore()
+    to_peers(
+        lambda d: pl.semaphore_signal(barrier, inc=1, device_id=(part, d), device_id_type=MESH)
+    )
+
+    page = lax.broadcasted_iota(i32, (MAXP, tokens), 1) // PAGE
+    slot_at = lax.broadcasted_iota(i32, (MAXP, tokens), 0)
+    offset = lax.broadcasted_iota(i32, (MAXP, tokens), 1) % PAGE
+    position = (slot_at * PAGE + offset).astype(f32)
+    eye = lax.broadcasted_iota(i32, (MAXP, MAXP), 0) == lax.broadcasted_iota(i32, (MAXP, MAXP), 1)
+    table = table_ref[...].astype(f32)
+    seen = []
+    for r in range(2):
+        pages = jnp.sum(jnp.where(eye, table[r : r + 1, :], 0.0), axis=1, keepdims=True)
+        length = len_ref[r].astype(f32)
+        hit = jnp.where((page.astype(f32) == pages) & (position < length), 1.0, 0.0)
+        seen.append(jnp.sum(hit, axis=0, keepdims=True))
+    row_of = (lax.broadcasted_iota(i32, (32, 1), 0) // 8) % 2
+    visible = jnp.where(row_of == 0, seen[0], seen[1])
+    bias[...] = jnp.where(visible > 0.5, 0.0, -1e30)
+
+    pl.semaphore_wait(barrier, n - 1)
+
+    def send1_copy(d):
+        return pltpu.make_async_remote_copy(
+            src_ref=send1.at[d],
+            dst_ref=recv1.at[me],
+            send_sem=ss1.at[d],
+            recv_sem=rs1.at[me],
+            device_id=(part, d),
+            device_id_type=MESH,
+        )
+
+    scale = HEAD_SIZE ** (-0.5)
+
+    def attend(g):
+        kv_copy(g).wait()
+        query = q_ref[pl.ds(pl.multiple_of(g * 32, 32), 32), :]
+        keys = kv[g, :, 0:128]
+        scores = lax.dot_general(query, keys, (((1,), (1,)), ((), ())), preferred_element_type=f32)
+        scores = scores * scale + bias[...]
+        fresh = new_ref[:, pl.ds(pl.multiple_of(g * 256, 256), 256)].astype(f32)
+        fresh = jnp.where(row_of == 0, fresh[0:1], fresh[1:2])
+        fresh_score = jnp.sum(query.astype(f32) * fresh[:, :128], axis=1, keepdims=True) * scale
+        top = jnp.maximum(jnp.max(scores, axis=1, keepdims=True), fresh_score)
+        grown = jnp.exp(scores - top)
+        fresh_grown = jnp.exp(fresh_score - top)
+        inverse = 1.0 / (jnp.sum(grown, axis=1, keepdims=True) + fresh_grown)
+        weights = (grown * inverse).astype(bf16)
+        fresh_weight = (fresh_grown * inverse).astype(bf16).astype(f32)
+        attended = jnp.dot(weights, kv[g, :, 128:256], preferred_element_type=f32)
+        attended = (attended + fresh_weight * fresh[:, 128:]).astype(bf16)
+        for half in range(2):
+            d = g * 2 + half
+            send1[d] = attended[half * 16 : half * 16 + 16]
+
+            @pl.when(d != me)
+            def _():
+                send1_copy(d).start()
+
+    loop(0, KVH, attend)
+
+    lane = lax.broadcasted_iota(i32, (rows, 128), 1) % rows
+    sub = lax.broadcasted_iota(i32, (rows, 128), 0)
+    owner_row = jnp.zeros((rows, 128), i32)
+    owner_column = jnp.zeros((rows, 128), i32)
+    for r in range(rows):
+        owner = storage_ref[adapter_ref[r, 0]]
+        owner_row = jnp.where(lane == r, owner, owner_row)
+        owner_column = jnp.where(sub == r, owner, owner_column)
+    same = owner_row == owner_column
+    first = lax.broadcasted_iota(i32, (rows, 128), 1) < rows
+    rank_row = jnp.sum(jnp.where(same & (sub < lane), 1.0, 0.0), axis=0, keepdims=True)
+    rank_column = jnp.sum(jnp.where(same & (lane < sub) & first, 1.0, 0.0), axis=1, keepdims=True)
+    slot_row = owner_row[0:1].astype(f32) * CAP + rank_row
+    slot_column = owner_column[:, 0:1].astype(f32) * CAP + rank_column
+    at = lax.broadcasted_iota(i32, (n * 16, 128), 0)
+    quarter_at = lax.broadcasted_iota(i32, (n * 16, 128), 1) // rows
+    wanted = ((at // 16) * CAP + at % CAP).astype(f32)
+    place = jnp.where((wanted == slot_row) & ((at // CAP) % 4 == quarter_at), 1.0, 0.0).astype(bf16)
+
+    recv1[me] = send1[me]
+    to_peers(lambda d: pltpu.make_async_remote_copy(
+        src_ref=send1.at[d],
+        dst_ref=recv1.at[d],
+        send_sem=ss1.at[d],
+        recv_sem=rs1.at[d],
+        device_id=(part, d),
+        device_id_type=MESH,
+    ).wait_recv())
+    xf[...] = recv1[...].reshape(n * 16, 128).astype(f32)
+    x = jnp.concatenate([xf[pl.ds(h, rows, stride=8), :] for h in range(8)], axis=1).astype(bf16)
+    xs[...] = x
+
+    def copy_of(send, recv, ss, rs, d, landing):
+        return pltpu.make_async_remote_copy(
+            src_ref=send.at[d],
+            dst_ref=recv.at[landing],
+            send_sem=ss.at[d],
+            recv_sem=rs.at[landing],
+            device_id=(part, d),
+            device_id_type=MESH,
+        )
+
+    stacked = jnp.concatenate([x[:, i * 256 : i * 256 + 256] for i in range(4)], axis=0)
+    picked = jnp.dot(place, stacked, preferred_element_type=f32).astype(bf16)
+    send2[...] = picked.reshape(n, 16, 256)
+    to_peers(lambda d: copy_of(send2, recv2, ss2, rs2, d, me).start())
+    recv2[me] = send2[me]
+
+    def partner_copy(k):
+        return pltpu.make_async_remote_copy(
+            src_ref=psend.at[k],
+            dst_ref=precv.at[k],
+            send_sem=pss.at[k],
+            recv_sem=prs.at[k],
+            device_id=(part, chip * 2 + 1 - core),
+            device_id_type=MESH,
+        )
+
+    def chip_copy(k):
+        return pltpu.make_async_remote_copy(
+            src_ref=isend.at[k],
+            dst_ref=irecv.at[k],
+            send_sem=iss.at[k],
+            recv_sem=irs.at[k],
+            device_id=(part, to_chip(k) * 2 + core),
+            device_id_type=MESH,
+        )
+
+    def multiply(k):
+        for own, into in ((0, psend), (1, keep)):
+            w_copy(k * 2 + own).wait()
+            for c in range(0, width, 512):
+                into[k, :, c : c + 512] = jnp.dot(
+                    xs[...], w[k * 2 + own, :, c : c + 512], preferred_element_type=f32
+                )
+            if own == 0:
+                partner_copy(k).start()
+
+    def finish(k):
+        partner_copy(k).wait_recv()
+        isend[k] = (keep[k] + precv[k]).astype(bf16)
+        chip_copy(k).start()
+
+    def step(k):
+        multiply(k)
+        finish(k - 1)
+
+    multiply(0)
+    loop(1, 4, step)
+
+    down_copy.wait()
+    up_copy.wait()
+    to_peers(lambda d: copy_of(send2, recv2, ss2, rs2, d, d).wait_recv())
+    quarter = lax.broadcasted_iota(i32, (16, 256), 0) // CAP
+
+    def reduce_one(s, total):
+        piece = recv2[s].astype(f32)
+        spread = jnp.concatenate(
+            [jnp.where(quarter == i, piece, 0.0) for i in range(4)], axis=1
+        ).astype(bf16)
+        factor = down[:, pl.ds(pl.multiple_of(s * width, width), width)]
+        return total + lax.dot_general(
+            spread, factor, (((1,), (1,)), ((), ())), preferred_element_type=f32
+        )
+
+    total = lax.fori_loop(0, n, reduce_one, jnp.zeros((16, down.shape[0]), f32))
+    summed = total[0:4] + total[4:8] + total[8:12] + total[12:16]
+    reduced = jnp.concatenate([summed] * 4, axis=0).astype(bf16)
+
+    def raise_one(d):
+        factor = up[:, pl.ds(pl.multiple_of(d * width, width), width)]
+        term = adapter_scale * jnp.dot(reduced, factor, preferred_element_type=f32)
+        piece = jnp.zeros((16, 256), f32)
+        for i in range(4):
+            piece = jnp.where(quarter == i, term[:, i * 256 : i * 256 + 256], piece)
+        send3[d] = piece.astype(bf16)
+
+        @pl.when(d != me)
+        def _():
+            copy_of(send3, recv3, ss3, rs3, d, me).start()
+
+    loop(0, n, raise_one)
+    recv3[me] = send3[me]
+
+    loop(4, chips, step)
+
+    to_peers(lambda d: copy_of(send3, recv3, ss3, rs3, d, d).wait_recv())
+    back = lax.broadcasted_iota(i32, (rows, n * 16), 1)
+    named = ((back // 16) * CAP + back % CAP).astype(f32) == slot_column
+    deltas = recv3[...].reshape(n * 16, 256)
+    last = chips - 1
+    partner_copy(last).wait_recv()
+    result = keep[last] + precv[last]
+    result = result + jnp.concatenate(
+        [
+            jnp.dot(
+                jnp.where(named & ((back // CAP) % 4 == i), 1.0, 0.0).astype(bf16),
+                deltas,
+                preferred_element_type=f32,
+            )
+            for i in range(4)
+        ],
+        axis=1,
+    )
+    for k in range(chips - 1):
+        chip_copy(k).wait_recv()
+        result = result + irecv[k].astype(f32)
+    out_ref[...] = result.astype(bf16)
+
+    def sent(d):
+        copy_of(send1, recv1, ss1, rs1, d, me).wait_send()
+        copy_of(send2, recv2, ss2, rs2, d, me).wait_send()
+        copy_of(send3, recv3, ss3, rs3, d, me).wait_send()
+
+    to_peers(sent)
+    loop(0, chips, lambda k: partner_copy(k).wait_send())
+    loop(0, chips - 1, lambda k: chip_copy(k).wait_send())
+
+
+def fused_body(
+    n,
+    queries,
+    new_token_key_value,
+    key_value_cache,
+    row_page_table,
+    lengths,
+    output_weight_matrix,
+    row_adapter_index,
+    adapter_storage_index,
+    adapter_down_factor,
+    adapter_up_factor,
+):
+    rows = row_adapter_index.shape[0]
+    width = output_weight_matrix.shape[0]
+    tokens = key_value_cache.shape[0] * PAGE
+    rank = adapter_down_factor.shape[1]
+    features = queries.shape[1]
+    chips = n // 2
+    heads = queries.reshape(2, n, 8, HEAD_SIZE).transpose(1, 0, 2, 3).reshape(n * 16, HEAD_SIZE)
+    bf16, f32 = jnp.bfloat16, jnp.float32
+    vmem = pl.BlockSpec(memory_space=pltpu.VMEM)
+    smem = pl.BlockSpec(memory_space=pltpu.SMEM)
+    hbm = pl.BlockSpec(memory_space=pl.ANY)
+    dma = pltpu.SemaphoreType.DMA
+    return pl.pallas_call(
+        functools.partial(fused_kernel, n),
+        out_shape=jax.ShapeDtypeStruct((rows, width), bf16),
+        in_specs=[vmem, vmem, hbm, vmem, smem, hbm, smem, smem, hbm, hbm],
+        out_specs=vmem,
+        scratch_shapes=[
+            pltpu.VMEM((KVH, tokens, 256), bf16),
+            pltpu.VMEM((n, width, width), bf16),
+            pltpu.VMEM((rank, features), bf16),
+            pltpu.VMEM((rank, features), bf16),
+            pltpu.VMEM((32, tokens), f32),
+            pltpu.VMEM((n, 16, 128), bf16),
+            pltpu.VMEM((n, 16, 128), bf16),
+            pltpu.VMEM((n * 16, 128), f32),
+            pltpu.VMEM((rows, width), bf16),
+            pltpu.VMEM((n, 16, 256), bf16),
+            pltpu.VMEM((n, 16, 256), bf16),
+            pltpu.VMEM((n, 16, 256), bf16),
+            pltpu.VMEM((n, 16, 256), bf16),
+            pltpu.VMEM((chips, rows, width), f32),
+            pltpu.VMEM((chips, rows, width), f32),
+            pltpu.VMEM((chips, rows, width), f32),
+            pltpu.VMEM((chips, rows, width), bf16),
+            pltpu.VMEM((chips, rows, width), bf16),
+            dma((KVH,)),
+            dma((n,)),
+            dma((2,)),
+            dma((n,)),
+            dma((n,)),
+            dma((n,)),
+            dma((n,)),
+            dma((n,)),
+            dma((n,)),
+            dma((chips,)),
+            dma((chips,)),
+            dma((chips,)),
+            dma((chips,)),
+        ],
+        compiler_params=pltpu.CompilerParams(
+            collective_id=0, has_side_effects=True, vmem_limit_bytes=56 * 1024 * 1024
+        ),
+    )(
+        heads,
+        new_token_key_value,
+        key_value_cache.reshape(tokens, key_value_cache.shape[2]),
+        row_page_table,
+        lengths,
+        output_weight_matrix,
+        row_adapter_index,
+        adapter_storage_index,
+        adapter_down_factor.reshape(rank, features),
+        adapter_up_factor.reshape(rank, features),
+    )
 
 
 def attend_rows(queries, new_token_key_value, gathered_pages, lengths):
@@ -96,4 +492,6 @@
         P(("parts", "tp"), None, None),
     )
     out_specs = P("parts", "tp")
-    return jax.shard_map(body, mesh=mesh, in_specs=in_specs, out_specs=out_specs, check_vma=False)
+    n = mesh.shape["tp"]
+    run = functools.partial(fused_body, n) if n == 16 else body
+    return jax.shard_map(run, mesh=mesh, in_specs=in_specs, out_specs=out_specs, check_vma=False)

time: 443 us -> 41.2 us (0.09)
  other arithmetic: 184 us -> 0 us
  local copies, waits for them, and re-layouts: 118 us -> 4.3 us
  blocking collectives: 70.3 us -> 0 us
  Pallas kernels: 0 us -> 36.5 us
  matrix products: 28 us -> 0 us
  starting transfers between devices: 19.7 us -> 0 us
  between operations: 13.6 us -> 0.01 us
  waiting for transfers between devices: 7.05 us -> 0 us
    unnamed x2 -> x0, other arithmetic: 182 us -> none
    unnamed x22 -> x3, local copies, waits for them, and re-layouts: 78 us -> 3.66 us
    psum x1 -> x0, blocking collectives: 70.3 us -> none  [body(): reduced_output = lax.psum(partial_low, 'tp').astype(jnp.bfloat16)]
    pallas_call x0 -> x1, Pallas kernels: none -> 36.5 us  [fused_body(): pl.pallas_call(functools.partial(fused_kernel, n), out_shape=jax.ShapeDty...]
    dot_general x6 -> x0, matrix products: 28 us -> none  [the longest x1 14.9 us: body(): jnp.dot(head_rows, output_weight_matrix, preferred_element_type=jnp.float32)]
    all_to_all x3 -> x0, starting transfers between devices: 19.5 us -> none  [the longest x1 7.39 us: body(): lax.all_to_all(attention_output, 'tp', split_axis=1, concat_axis=0, tiled...]
    gather x4 -> x0, local copies, waits for them, and re-layouts: 12.8 us -> none  [the longest x1 4.97 us: body(): gathered_pages = key_value_cache[row_page_table]]
    slice x1 -> x0, local copies, waits for them, and re-layouts: 10 us -> none  [attend_rows(): cached[:, :, :, 0, :]]
  transfers between devices with their start and end apart: 4 -> 0, of which waited for: 1 -> 0; matrix products, arithmetic and copies ran while one was open for 67% -> 0% of each run, Pallas kernels for 0% -> 0%
where the time goes in v1:
time: 41.2 us; the launch traced here: 40.8 us
  Pallas kernels  36.5 us (89%)
  local copies, waits for them, and re-layouts  4.3 us (10%)
    pallas_call x1, Pallas kernels, fused_body(): pl.pallas_call(functools.partial(fused_kernel, n), out_shape=jax.ShapeDty...  36.5 us
    unnamed x3, local copies, waits for them, and re-layouts  3.66 us

profile of v1, /device:TPU:0, one launch (start us, length us, event | category | flops | bytes accessed | tf_op | source)
XLA Modules:
  0.0 40.8 jit_solution(1932078543936327858)
XLA Ops:
  0.0 1.3 %copy.12.adapter_ref = s32[32,1]{1,0:T(8,128)} copy(s32[32,1]{0,1:T(1,128)} %param.16) | data formatting | bytes 256 | tf_op args[6]
  1.3 0.8 %copy.15 = bf16[1,2,128,128]{3,2,1,0:T(8,128)(2,1)S(1)} copy(bf16[1,2,128,128]{3,1,2,0:T(2,128)(2,1)} %bitcast.16) | data formatting | bytes 131072
  2.2 0.6 %copy.11 = bf16[2,16,8,128]{3,2,0,1:T(8,128)(2,1)} copy(bf16[2,16,8,128]{3,2,1,0:T(8,128)(2,1)S(1)} %bitcast.15) | data formatting | bytes 131072 | tf_op jit(solution)/shard_map/reshape | solution.py:351
  2.8 36.5 %shard_map.100 = bf16[32,1024]{1,0:T(8,128)(2,1)} custom-call(bf16[256,128]{1,0:T(8,128)(2,1)} %bitcast.14, bf16[2,2048]{1,0:T(2,128)(2,1)} %new_ref.1, bf16[1024,2048]{1,0:T(8,128)(2,1)} %bitcast.11, s32[2,32]{1,0:T(2,128)} %table_ref.1, s32[2]{0:T(128)} %len_ref.1, bf16[1024,16384]{1,0:T(8,128)(2,1)} %w_hbm.1, s32[32,1]{1,0:T(8,128)} %copy.12.adapter_ref, ...), custom_call_target="tpu_custom_call" | custom-call | tf_op jit(solution)/shard_map/pallas_call | solution.py:357
  39.3 1.5 %copy.17 = bf16[32,1024]{1,0:T(8,128)(2,1)} copy(bf16[32,1024]{1,0:T(8,128)(2,1)} %shard_map.100) | data formatting | bytes 131072

commit v2 on v1

--- a/solution.py
+++ b/solution.py
@@ -37,6 +37,7 @@
     down,
     up,
     bias,
+    qs,
     send1,
     recv1,
     xf,
@@ -48,6 +49,8 @@
     psend,
     precv,
     keep,
+    ysend,
+    yrecv,
     isend,
     irecv,
     kv_sem,
@@ -61,6 +64,8 @@
     rs3,
     pss,
     prs,
+    yss,
+    yrs,
     iss,
     irs,
 ):
@@ -69,13 +74,19 @@
     me = lax.axis_index("tp")
     core = lax.rem(me, 2)
     chip = lax.div(me, 2)
+    depth, across = lax.div(chip, 2), lax.rem(chip, 2)
     chips = n // 2
+    depths = chips // 2
     tokens = kv.shape[1]
     rows = xs.shape[0]
     width = xs.shape[1]
 
+    def to_depth(k):
+        return lax.rem(depth + k + 1, depths)
+
     def to_chip(k):
-        return lax.rem(chip + k + 1, chips)
+        near = lax.div(k, depths) == 1
+        return to_depth(lax.rem(k, depths)) * 2 + jnp.where(near, across, 1 - across)
 
     def kv_copy(g):
         return pltpu.make_async_copy(
@@ -103,15 +114,15 @@
         loop(0, n, one)
 
     loop(0, KVH, lambda g: kv_copy(g).start())
+    barrier = pltpu.get_barrier_semaphore()
+    to_peers(
+        lambda d: pl.semaphore_signal(barrier, inc=1, device_id=(part, d), device_id_type=MESH)
+    )
+
     loop(0, 8, lambda i: w_copy(i).start())
     down_copy.start()
     up_copy.start()
     loop(8, n, lambda i: w_copy(i).start())
-
-    barrier = pltpu.get_barrier_semaphore()
-    to_peers(
-        lambda d: pl.semaphore_signal(barrier, inc=1, device_id=(part, d), device_id_type=MESH)
-    )
 
     page = lax.broadcasted_iota(i32, (MAXP, tokens), 1) // PAGE
     slot_at = lax.broadcasted_iota(i32, (MAXP, tokens), 0)
@@ -129,7 +140,9 @@
     visible = jnp.where(row_of == 0, seen[0], seen[1])
     bias[...] = jnp.where(visible > 0.5, 0.0, -1e30)
 
-    pl.semaphore_wait(barrier, n - 1)
+    for h in range(n * 8):
+        at_row = (h // 8) * 16 + h % 8
+        qs[pl.ds(at_row, 2, stride=8), :] = q_ref[:, h * 128 : h * 128 + 128].astype(f32)
 
     def send1_copy(d):
         return pltpu.make_async_remote_copy(
@@ -145,7 +158,7 @@
 
     def attend(g):
         kv_copy(g).wait()
-        query = q_ref[pl.ds(pl.multiple_of(g * 32, 32), 32), :]
+        query = qs[pl.ds(pl.multiple_of(g * 32, 32), 32), :].astype(bf16)
         keys = kv[g, :, 0:128]
         scores = lax.dot_general(query, keys, (((1,), (1,)), ((), ())), preferred_element_type=f32)
         scores = scores * scale + bias[...]
@@ -164,18 +177,16 @@
             d = g * 2 + half
             send1[d] = attended[half * 16 : half * 16 + 16]
 
-            @pl.when(d != me)
-            def _():
-                send1_copy(d).start()
-
     loop(0, KVH, attend)
+    pl.semaphore_wait(barrier, n - 1)
+    to_peers(lambda d: send1_copy(d).start())
 
     lane = lax.broadcasted_iota(i32, (rows, 128), 1) % rows
     sub = lax.broadcasted_iota(i32, (rows, 128), 0)
     owner_row = jnp.zeros((rows, 128), i32)
     owner_column = jnp.zeros((rows, 128), i32)
     for r in range(rows):
-        owner = storage_ref[adapter_ref[r, 0]]
+        owner = storage_ref[adapter_ref[r]]
         owner_row = jnp.where(lane == r, owner, owner_row)
         owner_column = jnp.where(sub == r, owner, owner_column)
     same = owner_row == owner_column
@@ -228,13 +239,23 @@
             device_id_type=MESH,
         )
 
-    def chip_copy(k):
+    def across_copy(k):
+        return pltpu.make_async_remote_copy(
+            src_ref=ysend.at[k],
+            dst_ref=yrecv.at[k],
+            send_sem=yss.at[k],
+            recv_sem=yrs.at[k],
+            device_id=(part, (depth * 2 + 1 - across) * 2 + core),
+            device_id_type=MESH,
+        )
+
+    def depth_copy(k):
         return pltpu.make_async_remote_copy(
             src_ref=isend.at[k],
             dst_ref=irecv.at[k],
             send_sem=iss.at[k],
             recv_sem=irs.at[k],
-            device_id=(part, to_chip(k) * 2 + core),
+            device_id=(part, (to_depth(k) * 2 + across) * 2 + core),
             device_id_type=MESH,
         )
 
@@ -248,17 +269,31 @@
             if own == 0:
                 partner_copy(k).start()
 
-    def finish(k):
+    def sum_far(k):
         partner_copy(k).wait_recv()
-        isend[k] = (keep[k] + precv[k]).astype(bf16)
-        chip_copy(k).start()
-
-    def step(k):
+        ysend[k] = (keep[k] + precv[k]).astype(bf16)
+        across_copy(k).start()
+
+    def sum_near(k):
+        partner_copy(depths + k).wait_recv()
+        across_copy(k).wait_recv()
+        return keep[depths + k] + precv[depths + k] + yrecv[k].astype(f32)
+
+    def send_depth(k):
+        isend[k] = sum_near(k).astype(bf16)
+        depth_copy(k).start()
+
+    def far_step(k):
         multiply(k)
-        finish(k - 1)
+        sum_far(k - 1)
+
+    def near_step(k):
+        multiply(depths + k)
+        send_depth(k - 1)
 
     multiply(0)
-    loop(1, 4, step)
+    loop(1, depths + 1, far_step)
+    loop(1, depths - 1, near_step)
 
     down_copy.wait()
     up_copy.wait()
@@ -275,34 +310,38 @@
             spread, factor, (((1,), (1,)), ((), ())), preferred_element_type=f32
         )
 
-    total = lax.fori_loop(0, n, reduce_one, jnp.zeros((16, down.shape[0]), f32))
+    total = lax.fori_loop(0, n, reduce_one, jnp.zeros((16, down.shape[0]), f32), unroll=4)
     summed = total[0:4] + total[4:8] + total[8:12] + total[12:16]
     reduced = jnp.concatenate([summed] * 4, axis=0).astype(bf16)
 
-    def raise_one(d):
-        factor = up[:, pl.ds(pl.multiple_of(d * width, width), width)]
-        term = adapter_scale * jnp.dot(reduced, factor, preferred_element_type=f32)
-        piece = jnp.zeros((16, 256), f32)
-        for i in range(4):
-            piece = jnp.where(quarter == i, term[:, i * 256 : i * 256 + 256], piece)
-        send3[d] = piece.astype(bf16)
-
-        @pl.when(d != me)
-        def _():
-            copy_of(send3, recv3, ss3, rs3, d, me).start()
-
-    loop(0, n, raise_one)
+    send_depth(depths - 2)
+
+    def raise_four(start):
+        for d in [start * 4 + i for i in range(4)]:
+            factor = up[:, pl.ds(pl.multiple_of(d * width, width), width)]
+            term = adapter_scale * jnp.dot(reduced, factor, preferred_element_type=f32)
+            piece = jnp.zeros((16, 256), f32)
+            for i in range(4):
+                piece = jnp.where(quarter == i, term[:, i * 256 : i * 256 + 256], piece)
+            send3[d] = piece.astype(bf16)
+        for d in [start * 4 + i for i in range(4)]:
+
+            @pl.when(d != me)
+            def _():
+                copy_of(send3, recv3, ss3, rs3, d, me).start()
+
+    loop(0, n // 4, raise_four)
     recv3[me] = send3[me]
-
-    loop(4, chips, step)
+    multiply(chips - 1)
+    result = sum_near(depths - 1)
+    for k in range(depths - 1):
+        depth_copy(k).wait_recv()
+        result = result + irecv[k].astype(f32)
 
     to_peers(lambda d: copy_of(send3, recv3, ss3, rs3, d, d).wait_recv())
     back = lax.broadcasted_iota(i32, (rows, n * 16), 1)
     named = ((back // 16) * CAP + back % CAP).astype(f32) == slot_column
     deltas = recv3[...].reshape(n * 16, 256)
-    last = chips - 1
-    partner_copy(last).wait_recv()
-    result = keep[last] + precv[last]
     result = result + jnp.concatenate(
         [
             jnp.dot(
@@ -314,9 +353,6 @@
         ],
         axis=1,
     )
-    for k in range(chips - 1):
-        chip_copy(k).wait_recv()
-        result = result + irecv[k].astype(f32)
     out_ref[...] = result.astype(bf16)
 
     def sent(d):
@@ -326,7 +362,8 @@
 
     to_peers(sent)
     loop(0, chips, lambda k: partner_copy(k).wait_send())
-    loop(0, chips - 1, lambda k: chip_copy(k).wait_send())
+    loop(0, depths, lambda k: across_copy(k).wait_send())
+    loop(0, depths - 1, lambda k: depth_copy(k).wait_send())
 
 
 def fused_body(
@@ -348,7 +385,6 @@
     rank = adapter_down_factor.shape[1]
     features = queries.shape[1]
     chips = n // 2
-    heads = queries.reshape(2, n, 8, HEAD_SIZE).transpose(1, 0, 2, 3).reshape(n * 16, HEAD_SIZE)
     bf16, f32 = jnp.bfloat16, jnp.float32
     vmem = pl.BlockSpec(memory_space=pltpu.VMEM)
     smem = pl.BlockSpec(memory_space=pltpu.SMEM)
@@ -365,6 +401,7 @@
             pltpu.VMEM((rank, features), bf16),
             pltpu.VMEM((rank, features), bf16),
             pltpu.VMEM((32, tokens), f32),
+            pltpu.VMEM((n * 16, 128), f32),
             pltpu.VMEM((n, 16, 128), bf16),
             pltpu.VMEM((n, 16, 128), bf16),
             pltpu.VMEM((n * 16, 128), f32),
@@ -376,8 +413,10 @@
             pltpu.VMEM((chips, rows, width), f32),
             pltpu.VMEM((chips, rows, width), f32),
             pltpu.VMEM((chips, rows, width), f32),
-            pltpu.VMEM((chips, rows, width), bf16),
-            pltpu.VMEM((chips, rows, width), bf16),
+            pltpu.VMEM((chips // 2, rows, width), bf16),
+            pltpu.VMEM((chips // 2, rows, width), bf16),
+            pltpu.VMEM((chips // 2, rows, width), bf16),
+            pltpu.VMEM((chips // 2, rows, width), bf16),
             dma((KVH,)),
             dma((n,)),
             dma((2,)),
@@ -389,20 +428,22 @@
             dma((n,)),
             dma((chips,)),
             dma((chips,)),
-            dma((chips,)),
-            dma((chips,)),
+            dma((chips // 2,)),
+            dma((chips // 2,)),
+            dma((chips // 2,)),
+            dma((chips // 2,)),
         ],
         compiler_params=pltpu.CompilerParams(
             collective_id=0, has_side_effects=True, vmem_limit_bytes=56 * 1024 * 1024
         ),
     )(
-        heads,
+        queries,
         new_token_key_value,
         key_value_cache.reshape(tokens, key_value_cache.shape[2]),
         row_page_table,
         lengths,
         output_weight_matrix,
-        row_adapter_index,
+        row_adapter_index.reshape(rows),
         adapter_storage_index,
         adapter_down_factor.reshape(rank, features),
         adapter_up_factor.reshape(rank, features),

time: 41.2 us -> 33.9 us (0.82)
  Pallas kernels: 36.5 us -> 32.3 us
  local copies, waits for them, and re-layouts: 4.3 us -> 1.47 us
    pallas_call x1, Pallas kernels: 36.5 us -> 32.3 us  [fused_body(): pl.pallas_call(functools.partial(fused_kernel, n), out_shape=jax.ShapeDty...]
    unnamed x3 -> x1, local copies, waits for them, and re-layouts: 3.66 us -> 1.47 us
    reshape x1 -> x0, local copies, waits for them, and re-layouts: 0.64 us -> none  [fused_body(): queries.reshape(2, n, 8, HEAD_SIZE).transpose(1, 0, 2, 3)]
where the time goes in v2:
time: 33.9 us; the launch traced here: 33.7 us
  Pallas kernels  32.3 us (95%)
  local copies, waits for them, and re-layouts  1.47 us (4%)
    pallas_call x1, Pallas kernels, fused_body(): pl.pallas_call(functools.partial(fused_kernel, n), out_shape=jax.ShapeDty...  32.3 us
    unnamed x1, local copies, waits for them, and re-layouts  1.47 us

profile of v2, /device:TPU:0, one launch (start us, length us, event | category | flops | bytes accessed | tf_op | source)
XLA Modules:
  0.0 33.7 jit_solution(16000981265951493181)
XLA Ops:
  0.0 32.3 %shard_map.100 = bf16[32,1024]{1,0:T(8,128)(2,1)} custom-call(bf16[2,16384]{1,0:T(2,128)(2,1)} %q_ref.1, bf16[2,2048]{1,0:T(2,128)(2,1)} %new_ref.1, bf16[1024,2048]{1,0:T(8,128)(2,1)} %bitcast.4, s32[2,32]{1,0:T(2,128)} %table_ref.1, s32[2]{0:T(128)} %len_ref.1, bf16[1024,16384]{1,0:T(8,128)(2,1)} %w_hbm.1, s32[32]{0:T(128)} %bitcast.7, s32[16]{0:T(128)} %storage_ref.1, ...), custom_call_target="tpu_custom_call" | custom-call | tf_op jit(solution)/shard_map/pallas_call | solution.py:393
  32.3 1.5 %copy.12 = bf16[32,1024]{1,0:T(8,128)(2,1)} copy(bf16[32,1024]{1,0:T(8,128)(2,1)} %shard_map.100) | data formatting | bytes 131072

commit v3 on v2

--- a/solution.py
+++ b/solution.py
@@ -82,7 +82,8 @@
     width = xs.shape[1]
 
     def to_depth(k):
-        return lax.rem(depth + k + 1, depths)
+        shift = jnp.where(k == 0, 2, jnp.where(k == 1, 1, jnp.where(k == 2, 3, 0)))
+        return lax.rem(depth + shift, depths)
 
     def to_chip(k):
         near = lax.div(k, depths) == 1
@@ -295,6 +296,9 @@
     loop(1, depths + 1, far_step)
     loop(1, depths - 1, near_step)
 
+    multiply(chips - 1)
+    send_depth(depths - 2)
+
     down_copy.wait()
     up_copy.wait()
     to_peers(lambda d: copy_of(send2, recv2, ss2, rs2, d, d).wait_recv())
@@ -313,8 +317,6 @@
     total = lax.fori_loop(0, n, reduce_one, jnp.zeros((16, down.shape[0]), f32), unroll=4)
     summed = total[0:4] + total[4:8] + total[8:12] + total[12:16]
     reduced = jnp.concatenate([summed] * 4, axis=0).astype(bf16)
-
-    send_depth(depths - 2)
 
     def raise_four(start):
         for d in [start * 4 + i for i in range(4)]:
@@ -332,7 +334,6 @@
 
     loop(0, n // 4, raise_four)
     recv3[me] = send3[me]
-    multiply(chips - 1)
     result = sum_near(depths - 1)
     for k in range(depths - 1):
         depth_copy(k).wait_recv()

time: 33.9 us -> 33.7 us (level)
  no operation moved by 1% of the time
where the time goes in v3:
time: 33.7 us; the launch traced here: 33.5 us
  Pallas kernels  32 us (95%)
  local copies, waits for them, and re-layouts  1.47 us (4%)
    pallas_call x1, Pallas kernels, fused_body(): pl.pallas_call(functools.partial(fused_kernel, n), out_shape=jax.ShapeDty...  32 us
    unnamed x1, local copies, waits for them, and re-layouts  1.47 us

profile of v3, /device:TPU:0, one launch (start us, length us, event | category | flops | bytes accessed | tf_op | source)
XLA Modules:
  0.0 33.5 jit_solution(13193744190200876269)
XLA Ops:
  0.0 32.0 %shard_map.100 = bf16[32,1024]{1,0:T(8,128)(2,1)} custom-call(bf16[2,16384]{1,0:T(2,128)(2,1)} %q_ref.1, bf16[2,2048]{1,0:T(2,128)(2,1)} %new_ref.1, bf16[1024,2048]{1,0:T(8,128)(2,1)} %bitcast.4, s32[2,32]{1,0:T(2,128)} %table_ref.1, s32[2]{0:T(128)} %len_ref.1, bf16[1024,16384]{1,0:T(8,128)(2,1)} %w_hbm.1, s32[32]{0:T(128)} %bitcast.7, s32[16]{0:T(128)} %storage_ref.1, ...), custom_call_target="tpu_custom_call" | custom-call | tf_op jit(solution)/shard_map/pallas_call | solution.py:394
  32.0 1.5 %copy.12 = bf16[32,1024]{1,0:T(8,128)(2,1)} copy(bf16[32,1024]{1,0:T(8,128)(2,1)} %shard_map.100) | data formatting | bytes 131072
